TPU v7x, 32 devices: a whole 2x2x4 slice. The times are simulated.
32 devices in a mesh: row: 4 (over x, core), col: 8 (over z, y).
Axes of the slice: x: 2, y: 2, z: 4, core: 2. Of those that a mesh axis runs over, the one named last changes fastest.
Arguments:
- vectors: bfloat16 [16, 32768], P(None, ('row', 'col')), may hold values from -6 to 6
- tiles: bfloat16 [4, 8, 8, 512, 512], P('row', 'col'), may hold values from -0.25 to 0.25
- block_rows: int32 [4, 8, 8], P('row', 'col'), may hold values from 0 to 15
- block_cols: int32 [4, 8, 8], P('row', 'col'), may hold values from 0 to 7
- counts: int32 [4, 8], P('row', 'col'), may hold values from 1 to 8, as said below
Outputs:
- hx: float32 [16, 32768], P(None, ('row', 'col'))
Inputs may be any that keep to these rules, and one draw needn't show every extreme that they name: `counts`: every tile has between 1 and 8 live blocks; in every draw one tile has all 8 slots live, the others at most half.
All inputs are finite; a program needn't handle non-finite values.
Results may differ from a plain program's by a relative error of at most 0.0003.
Values may be sent and summed in bfloat16 or wider, within the bound.
No kernel may reach another device: no remote copies, remote signals or barrier semaphores. Data moves between devices by JAX's collectives and lax.ppermute only.
A program may use at most 64 MiB of HBM per device.

v0:
```python
import jax
import jax.numpy as jnp
from jax import lax
from jax.sharding import PartitionSpec as P


def add_at(total, piece, start):
    width = piece.shape[1]
    old = lax.dynamic_slice_in_dim(total, start, width, 1)
    return lax.dynamic_update_slice_in_dim(total, old + piece, start, 1)


def sum_over_cols(partial_value):
    return lax.psum_scatter(partial_value, "col", scatter_dimension=1, tiled=True)


def sum_over_rows(partial_value):
    return lax.psum_scatter(partial_value, "row", scatter_dimension=1, tiled=True)


def on_device(vectors, tiles, block_rows, block_cols, counts):
    block_size = tiles.shape[-1]
    local_tiles = tiles[0, 0]
    row_local = block_rows[0, 0]
    col_local = block_cols[0, 0]
    live_count = counts[0, 0]
    row_vectors = lax.all_gather(vectors, "col", axis=1, tiled=True)
    col_vectors = lax.all_gather(vectors, "row", axis=1, tiled=True)
    row_total = jnp.zeros((vectors.shape[0], row_vectors.shape[1]), jnp.float32)
    col_total = jnp.zeros((vectors.shape[0], col_vectors.shape[1]), jnp.float32)

    def both_add(slot_index, totals):
        block = lax.dynamic_index_in_dim(local_tiles, slot_index, 0, keepdims=False)
        row_start = row_local[slot_index] * block_size
        col_start = col_local[slot_index] * block_size
        col_piece = lax.dynamic_slice_in_dim(col_vectors, col_start, block_size, 1)
        row_piece = lax.dynamic_slice_in_dim(row_vectors, row_start, block_size, 1)
        direct = lax.dot_general(
            col_piece, block, (((1,), (1,)), ((), ())), preferred_element_type=jnp.float32
        )
        mirror = jnp.dot(row_piece, block, preferred_element_type=jnp.float32)
        return (add_at(totals[0], direct, row_start), add_at(totals[1], mirror, col_start))

    totals = lax.fori_loop(0, live_count, both_add, (row_total, col_total))
    row_result = sum_over_cols(totals[0])
    col_result = sum_over_rows(totals[1])
    return row_result + col_result


def solution(mesh):
    placed = (
        P(None, ("row", "col")),
        P("row", "col", None, None, None),
        P("row", "col", None),
        P("row", "col", None),
        P("row", "col"),
    )
    return jax.shard_map(
        on_device, mesh=mesh, in_specs=placed, out_specs=P(None, ("row", "col")), check_vma=False
    )
```

profile of v0, /device:TPU:0, one launch (start us, length us, event | category | flops | bytes accessed | tf_op | source)
XLA Modules:
  0.0 188.6 jit_solution(4641537373821990921)
XLA Ops:
  6.5 0.0 reduce-scatter.5.cloned.1.call-start
  6.5 6.7 %all_gather.6 = bf16[16,4096]{1,0:T(8,128)(2,1)S(1)} all-gather(bf16[16,1024]{1,0:T(8,128)(2,1)} %param.7), channel_id=1, replica_groups=mesh['row'=4,'col'=8] {'row'}, dimensions={1}, use_global_device_ids=true | all-gather | bytes 163840 | tf_op jit(solution)/shard_map/all_gather | solution.py:28
  13.2 31.8 %all_gather.7 = bf16[16,8192]{1,0:T(8,128)(2,1)S(1)} all-gather(bf16[16,1024]{1,0:T(8,128)(2,1)} %param.7), channel_id=1, replica_groups=mesh['row'=4,'col'=8] {'col'}, dimensions={1}, use_global_device_ids=true | all-gather | bytes 294912 | tf_op jit(solution)/shard_map/all_gather | solution.py:27
  45.1 28.6 %while.12 = (s32[]{:T(128)}, f32[16,8192]{1,0:T(8,128)S(1)}, f32[16,4096]{1,0:T(8,128)S(1)}, s32[]{:T(128)}, s32[8]{0:T(128)}, /*index=5*/s32[8]{0:T(128)}, bf16...) while((s32[]{:T(128)}, f32[16,8192]{1,0:T(8,128)S(1)}, ...), condition=%wide.region_1.2_spmd, body=%wide.region_0.1_spmd.sunk | while | flops 16793612 | bytes 1212739 | solution.py:44
  45.8 1.3 dynamic_slice.50
  47.6 1.3 dynamic_slice.51
  49.5 1.2 fusion.21
  50.8 1.3 fusion.20
  52.7 1.3 dynamic_slice.50
  54.6 1.3 dynamic_slice.51
  56.5 1.2 fusion.21
  57.7 1.3 fusion.20
  59.7 1.3 dynamic_slice.50
  61.6 1.3 dynamic_slice.51
  63.5 1.2 fusion.21
  64.7 1.3 fusion.20
  66.7 1.3 dynamic_slice.50
  68.6 1.3 dynamic_slice.51
  70.5 1.2 fusion.21
  71.7 1.3 fusion.20
  73.7 0.0 copy-start.1
  73.7 0.0 copy-start
  73.7 0.7 copy-done.1
  74.4 0.0 reduce-scatter.5.cloned.1.call-update
  74.4 0.0 reduce-scatter.3.cloned.1.call-start
  74.4 0.1 copy-done
  74.5 0.6 reduce-scatter.3.cloned.1.call-update
  75.1 39.5 %reduce-scatter.5.cloned.1.call-done = f32[16,1024]{1,0:T(8,128)} async-done(((f32[16,4096]{1,0:T(8,128)}), f32[16,1024]{1,0:T(8,128)}) %reduce-scatter.5.cloned.1.call-update) | async-done | bytes 65552 | tf_op jit(solution)/shard_map/reduce_scatter | solution.py:18
  114.6 65.7 %reduce-scatter.3.cloned.1.call-done = f32[16,1024]{1,0:T(8,128)} async-done(((f32[16,8192]{1,0:T(8,128)}), f32[16,1024]{1,0:T(8,128)}) %reduce-scatter.3.cloned.1.call-update) | async-done | bytes 65552 | tf_op jit(solution)/shard_map/reduce_scatter | solution.py:14
  180.3 1.5 add.32
  (2 shorter events, 0.1 us)
Async XLA Ops:
  6.5 108.1 %reduce-scatter.5.cloned.1.call-start = ((), (), s32[]{:S(2)}) async-start(), calls=%async_computation.3 | async-start | bytes 327680 | tf_op jit(solution)/shard_map/reduce_scatter | solution.py:18
  73.7 0.7 copy-start.1
  73.7 0.9 copy-start
  74.4 105.9 %reduce-scatter.3.cloned.1.call-start = ((), (), s32[]{:S(2)}) async-start(), calls=%async_computation.2 | async-start | bytes 589824 | tf_op jit(solution)/shard_map/reduce_scatter | solution.py:14
Sparse Core Ops, SparseCore 0:
  74.5 40.0 reduce-scatter.4
  118.3 61.9 reduce-scatter.2
where the time goes:
time: 189 us
  waiting for transfers between devices  106 us (56%)
  blocking collectives  38.5 us (20%)
  between operations  13.4 us (7%)
  local copies, waits for them, and re-layouts  11 us (6%)
  matrix products  10 us (5%)
  loops' own time  8.35 us (4%)
    reduce_scatter x1, waiting for transfers between devices, sum_over_cols(): lax.psum_scatter(partial_value, 'col', scatter_dimension=1, tiled=True)  65.7 us
    reduce_scatter x1, waiting for transfers between devices, sum_over_rows(): lax.psum_scatter(partial_value, 'row', scatter_dimension=1, tiled=True)  39.5 us
    all_gather x1, blocking collectives, on_device(): row_vectors = lax.all_gather(vectors, 'col', axis=1, tiled=True)  31.8 us
    another operation x1, loops' own time, on_device(): totals = lax.fori_loop(0, live_count, both_add, (row_total, col_total))  8.35 us
    all_gather x1, blocking collectives, on_device(): col_vectors = lax.all_gather(vectors, 'row', axis=1, tiled=True)  6.68 us
    dot_general x4, matrix products, both_add(): lax.dot_general(col_piece, block, (((1,), (1,)), ((), ())), preferred_ele...  5.12 us
    dynamic_slice x4, local copies, waits for them, and re-layouts, both_add(): col_start = col_local[slot_index] * block_size  5.1 us
    dynamic_slice x4, local copies, waits for them, and re-layouts, both_add(): row_start = row_local[slot_index] * block_size  5.09 us
  transfers between devices with their start and end apart: 2, of which 2 were waited for; matrix products, arithmetic and copies ran while one was open for 0% of the time, Pallas kernels for 0%

commit v1 on v0

v1 whole, which is shorter than its diff:
```python
import functools

import jax
import jax.numpy as jnp
from jax import lax
from jax.experimental import pallas as pl
from jax.experimental.pallas import tpu as pltpu
from jax.sharding import PartitionSpec as P

F32 = jnp.float32
I16 = jnp.int16
LANES = 128
STEPS = 64.0
TOP = 32700.0
VMEM = pl.BlockSpec(memory_space=pltpu.VMEM)
SMEM = pl.BlockSpec(memory_space=pltpu.SMEM)
ANY = pl.BlockSpec(memory_space=pl.ANY)


def coded(total):
    biggest = jnp.max(jnp.abs(total), axis=1, keepdims=True)
    code = jnp.ceil(STEPS * jnp.log2(jnp.maximum(biggest, 2.0 ** -126)))
    scaled = total * jnp.exp2(code * (-1.0 / STEPS))
    return jnp.floor(scaled * TOP + 0.5).astype(jnp.int32).astype(I16), code


def write_piece(piece, totals):
    size, depth = totals[0].shape[1], len(totals)
    spot = lax.broadcasted_iota(jnp.int32, (totals[0].shape[0], LANES), 1)
    codes = jnp.zeros(spot.shape, F32)
    for k, total in enumerate(totals):
        values, code = coded(total)
        piece[:, k * size:(k + 1) * size] = values
        codes = jnp.where(spot >= k * (LANES // depth), code, codes)
    piece[:, depth * size:] = codes.astype(jnp.int32).astype(I16)


def read_piece(piece, depth):
    size = (piece.shape[1] - LANES) // depth
    codes = piece[:, depth * size:].astype(jnp.int32).astype(F32)
    scales = jnp.exp2(codes * (1.0 / STEPS)) * (1.0 / TOP)
    parts = []
    for k in range(depth):
        spot = k * (LANES // depth)
        part = piece[:, k * size:(k + 1) * size].astype(jnp.int32).astype(F32)
        parts.append(part * scales[:, spot:spot + 1])
    return parts


def mark(out):
    out[...] = jnp.zeros_like(out)


def stack_pieces(n_pieces, *refs):
    stack = refs[-1]
    for d, piece in enumerate(refs[:n_pieces][::-1]):
        stack[d] = piece[...]


def gathered_place(block, depth, me, size, nears, odd):
    apart, places = lax.bitwise_xor(block // depth, me), []
    for near in nears:
        at_far = apart % near + apart // (2 * near) * near
        places.append((apart // near % 2 * (size // 2) + at_far) * depth + block % depth)
    return jnp.where(odd, places[1], places[0])


def turned(distance, odd):
    low = 2 if odd else 1
    bits = distance // low % 2, distance // (2 * low) % 2
    return distance + (bits[1] - bits[0]) * low + (bits[0] - bits[1]) * 2 * low


def summed_place(apart, block, depth, n_far, part):
    return (apart % part * n_far + apart // part) * depth + block % depth


def load_pieces(x, *stacks):
    size, at = x.shape[2], 0
    for stack in stacks:
        for d in range(stack.shape[0]):
            for k in range(stack.shape[2] // size):
                x[at] = stack[d, :, k * size:(k + 1) * size]
                at += 1


def store_pieces(total, kept, *leaving):
    n_far, size = kept.shape[0], total.shape[2]
    depth = kept.shape[2] // size
    for d in range(n_far):
        for a, out in enumerate(leaving):
            at = ((len(leaving) - a) * n_far + d) * depth
            write_piece(out.at[d], [total[at + k] for k in range(depth)])
        for k in range(depth):
            kept[d, :, k * size:(k + 1) * size] = total[d * depth + k]


def work_blocks(index_ref, count_ref, held, x, total, find, contract):
    slots = held.shape[0]
    group = slots // 2 if slots % 2 == 0 else slots
    count = count_ref[0, 0]

    def work(at):
        parts = []
        for slot in range(at, at + group):
            source, target = find(index_ref[slot], index_ref[slots + slot])
            product = lax.dot_general(
                x[source], held[slot], (((1,), (contract,)), ((), ())), preferred_element_type=F32
            )
            parts.append((target, jnp.where(slot < count, product, 0.0)))
        for target, product in parts:
            total[target] += product

    total[...] = jnp.zeros_like(total)
    for at in range(0, slots, group):
        @pl.when(at < count)
        def _():
            work(at)


def direct_blocks(plan, index_ref, count_ref, tiles, *refs):
    pieces, (kept, *leaving), (x, total) = refs[:2], refs[2:-2], refs[-2:]
    held, depth = tiles.at[0, 0], kept.shape[2] // tiles.shape[-1]
    row_me, col_me = lax.axis_index("row"), lax.axis_index("col")
    odd = row_me % 2 == 1

    def find(p, q):
        apart = lax.bitwise_xor(p // depth, col_me)
        apart = jnp.where(odd, turned(apart, True), turned(apart, False))
        return (
            gathered_place(q, depth, row_me, x.shape[0] // depth, plan["row"][0], odd),
            summed_place(apart, p, depth, kept.shape[0], plan["col"][1]),
        )

    load_pieces(x, *pieces)
    work_blocks(index_ref, count_ref, held, x, total, find, 1)
    store_pieces(total, kept, *leaving)


def mirror_blocks(plan, index_ref, count_ref, tiles, *refs):
    pieces, (kept, *leaving), (x, total) = refs[:2], refs[3:-2], refs[-2:]
    held, depth = tiles.at[0, 0], kept.shape[2] // tiles.shape[-1]
    row_me, col_me = lax.axis_index("row"), lax.axis_index("col")
    odd = row_me % 2 == 1

    def find(p, q):
        apart = lax.bitwise_xor(q // depth, row_me)
        return (
            gathered_place(p, depth, col_me, x.shape[0] // depth, plan["col"][0], odd),
            summed_place(apart, q, depth, kept.shape[0], plan["row"][1]),
        )

    load_pieces(x, *pieces)
    work_blocks(index_ref, count_ref, held, x, total, find, 0)
    store_pieces(total, kept, *leaving)


def add_near(depth, kept, *refs):
    n_far = kept.shape[0]
    came, late, (mine, *far_out), late_out = refs[:-n_far - 2], refs[-n_far - 2], refs[-n_far - 1:-1], refs[-1]
    size = mine.shape[2] // depth
    cuts = [slice(k * size, (k + 1) * size) for k in range(depth)]
    for d in range(n_far):
        totals = [kept[d, :, cut] for cut in cuts]
        for piece in came:
            totals = [total + part for total, part in zip(totals, read_piece(piece.at[d], depth))]
        if d > 0:
            write_piece(far_out[d - 1].at[0], totals)
            continue
        for cut, total in zip(cuts, totals):
            mine[0, :, cut] = total
    late_out[...] = late[...]


def add_up(depth, n_sums, *refs):
    sums, came, result = refs[:n_sums], refs[n_sums:-1], refs[-1]
    size = result.shape[1] // depth
    cuts = [slice(k * size, (k + 1) * size) for k in range(depth)]
    totals = [sum(part[0, :, cut] for part in sums) for cut in cuts]
    for piece in came:
        totals = [total + part for total, part in zip(totals, read_piece(piece.at[0], depth))]
    for cut, total in zip(cuts, totals):
        result[:, cut] = total


def on_device(n_row, n_col, vectors, tiles, block_rows, block_cols, counts):
    vecs, width = vectors.shape
    slots, size = tiles.shape[2], tiles.shape[-1]
    depth = width // size
    sizes = {"row": n_row, "col": n_col}
    plan = {"row": ((1, 1), 4), "col": ((2, 1), 4)}
    far = {axis: n // plan[axis][1] for axis, n in sizes.items()}
    piece = jax.ShapeDtypeStruct((vecs, width + LANES), I16)
    whole = jax.ShapeDtypeStruct((vecs, width), F32)

    def many(n, one):
        return jax.ShapeDtypeStruct((n,) + one.shape, one.dtype)

    def swap(value, axis, apart):
        pairs = []
        for r in range(n_row):
            for c in range(n_col):
                to = (r ^ apart[r % 2], c) if axis == "row" else (r, c ^ apart[r % 2])
                pairs.append((r * n_col + c, to[0] * n_col + to[1]))
        return lax.ppermute(value, ("row", "col"), pairs)

    def gather_ways(axis):
        longest = range(sizes[axis] - 1, 0, -1)
        return list(zip(*([d for d in longest if not d & near] for near in plan[axis][0])))

    def ways(axis, distances):
        return [
            tuple(turned(d, odd) if axis == "col" else d for odd in (False, True)) for d in distances
        ]

    def near_ways(axis):
        return ways(axis, range(plan[axis][1] - 1, 0, -1))

    def far_ways(axis):
        part = plan[axis][1]
        return ways(axis, range(sizes[axis] - part, 0, -part))

    def small_call(body, outs, name, operands):
        total = sum(x.size * x.dtype.itemsize for x in list(outs) + list(operands))
        return pl.pallas_call(
            body,
            out_shape=outs,
            in_specs=[VMEM] * len(operands),
            out_specs=[VMEM] * len(outs),
            compiler_params=pltpu.CompilerParams(vmem_limit_bytes=2**21 + 2 * total),
            name=name,
        )(*operands)

    def block_call(body, axis_in, axis_out, pieces, name, after=()):
        return pl.pallas_call(
            functools.partial(body, plan),
            out_shape=[many(far[axis_out], whole)]
            + [many(far[axis_out], piece)] * (plan[axis_out][1] - 1),
            in_specs=[SMEM] * 2 + [VMEM] * 3 + [ANY] * len(after),
            out_specs=[VMEM] * plan[axis_out][1],
            scratch_shapes=[
                pltpu.VMEM((sizes[axis_in] * depth, vecs, size), vectors.dtype),
                pltpu.VMEM((sizes[axis_out] * depth, vecs, size), F32),
            ],
            compiler_params=pltpu.CompilerParams(vmem_limit_bytes=16 * 2**20),
            cost_estimate=pl.CostEstimate(
                flops=slots * 200 * vecs * size * size,
                bytes_accessed=slots * size * size * 16,
                transcendentals=0,
            ),
            name=name,
        )(index, counts, tiles, *pieces, *after)

    def stack(axis, *after):
        pieces = [got[axis, way] for way in gather_ways(axis)] + [vectors]
        body = functools.partial(stack_pieces, len(pieces))
        outs = [jax.ShapeDtypeStruct((len(pieces), vecs, width), vectors.dtype)]
        return small_call(body, outs, "stack_pieces", [*pieces, *after])[0]

    index = jnp.concatenate([block_rows[0, 0], block_cols[0, 0]])
    got = {
        (axis, way): swap(vectors, axis, way) for axis in ("row", "col") for way in gather_ways(axis)
    }
    marked = pl.pallas_call(
        mark,
        out_shape=jax.ShapeDtypeStruct((vecs, LANES), F32),
        out_specs=VMEM,
        compiler_params=pltpu.CompilerParams(vmem_limit_bytes=2**21),
        cost_estimate=pl.CostEstimate(
            flops=2 * 10**9, bytes_accessed=2**22, transcendentals=0
        ),
        name="mark",
    )()
    row_stack = stack("row", marked)
    row_pieces = [row_stack, swap(row_stack, "row", plan["row"][0])]
    col_kept, *leaving = block_call(direct_blocks, "row", "col", row_pieces, "direct_blocks")
    col_stack = stack("col", marked)
    col_pieces = [col_stack, swap(col_stack, "col", plan["col"][0])]
    col_came = [swap(out, "col", way) for out, way in zip(leaving, near_ways("col"))]
    row_kept, *leaving = block_call(
        mirror_blocks, "col", "row", col_pieces, "mirror_blocks", [col_kept]
    )
    *first, last = near_ways("row")
    row_came = [swap(out, "row", way) for out, way in zip(leaving, first)]

    col_kept, *far_out, late = small_call(
        functools.partial(add_near, depth),
        [many(1, whole)] + [many(1, piece)] * (far["col"] - 1) + [many(far["row"], piece)],
        "add_near",
        [col_kept, *col_came, leaving[-1]],
    )
    col_came = [swap(out, "col", way) for out, way in zip(far_out[::-1], far_ways("col"))]
    row_came.append(swap(late, "row", last))
    if far["row"] > 1:
        row_kept, *far_out, _ = small_call(
            functools.partial(add_near, depth),
            [many(1, whole)] + [many(1, piece)] * far["row"],
            "add_near",
            [row_kept, *row_came, col_came[0]],
        )
        row_came = [swap(out, "row", way) for out, way in zip(far_out[::-1], far_ways("row"))]
    sums = [col_kept, row_kept]
    body = functools.partial(add_up, depth, len(sums))
    return small_call(body, [whole], "add_up", [*sums, *col_came, *row_came])[0]


def solution(mesh):
    placed = (
        P(None, ("row", "col")),
        P("row", "col", None, None, None),
        P("row", "col", None),
        P("row", "col", None),
        P("row", "col"),
    )
    return jax.shard_map(
        functools.partial(on_device, mesh.shape["row"], mesh.shape["col"]),
        mesh=mesh,
        in_specs=placed,
        out_specs=P(None, ("row", "col")),
        check_vma=False,
    )
```

time: 189 us -> 27 us (0.14)
  waiting for transfers between devices: 106 us -> 7.17 us
  blocking collectives: 38.5 us -> 0 us
  starting transfers between devices: 0.04 us -> 15.4 us
  between operations: 13.4 us -> 0.73 us
  local copies, waits for them, and re-layouts: 11 us -> 0.01 us
  matrix products: 10 us -> 0 us
  loops' own time: 8.35 us -> 0 us
  Pallas kernels: 0 us -> 3.44 us
    reduce_scatter x2 -> x0, waiting for transfers between devices: 105 us -> none  [the longest x1 65.7 us: sum_over_cols(): lax.psum_scatter(partial_value, 'col', scatter_dimension=1, tiled=True)]
    all_gather x2 -> x0, blocking collectives: 38.5 us -> none  [the longest x1 31.8 us: on_device(): row_vectors = lax.all_gather(vectors, 'col', axis=1, tiled=True)]
    ppermute x0 -> x13, starting transfers between devices: none -> 15.4 us  [swap(): return lax.ppermute(value, ('row', 'col'), pairs)]
    dynamic_slice x8 -> x0, local copies, waits for them, and re-layouts: 10.2 us -> none  [the longest x4 5.1 us: both_add(): col_start = col_local[slot_index] * block_size]
    dot_general x8 -> x0, matrix products: 10 us -> none  [the longest x4 5.12 us: both_add(): lax.dot_general(col_piece, block, (((1,), (1,)), ((), ())), preferred_ele...]
    another operation x1 -> x0, loops' own time: 8.35 us -> none  [on_device(): totals = lax.fori_loop(0, live_count, both_add, (row_total, col_total))]
    ppermute x0 -> x13, waiting for transfers between devices: none -> 7.17 us  [swap(): return lax.ppermute(value, ('row', 'col'), pairs)]
    pallas_call x0 -> x7, Pallas kernels: none -> 3.44 us  [the longest x2 2.5 us: block_call(): pl.pallas_call(functools.partial(body, plan), out_shape=[many(far[axis_ou...]
  transfers between devices with their start and end apart: 2 -> 13, of which waited for: 2 -> 7; matrix products, arithmetic and copies ran while one was open for 0% -> 0% of each run, Pallas kernels for 0% -> 10%
where the time goes in v1:
time: 27 us; the launch traced here: 26.9 us
  starting transfers between devices  15.4 us (57%)
  waiting for transfers between devices  7.17 us (27%)
  Pallas kernels  3.44 us (13%)
  between operations  0.73 us (3%)
    ppermute x13, starting transfers between devices, swap(): return lax.ppermute(value, ('row', 'col'), pairs)  15.4 us
    ppermute x13, waiting for transfers between devices, swap(): return lax.ppermute(value, ('row', 'col'), pairs)  7.17 us
    pallas_call x2, Pallas kernels, block_call(): pl.pallas_call(functools.partial(body, plan), out_shape=[many(far[axis_ou...  2.5 us
    pallas_call x4, Pallas kernels, small_call(): pl.pallas_call(body, out_shape=outs, in_specs=[VMEM] * len(operands), out...  0.95 us
  transfers between devices with their start and end apart: 13, of which 7 were waited for; matrix products, arithmetic and copies ran while one was open for 0% of the time, Pallas kernels for 10%

profile of v1, /device:TPU:0, one launch (start us, length us, event | category | flops | bytes accessed | tf_op | source)
XLA Modules:
  0.0 26.9 jit_solution(7526985916189078343)
XLA Ops:
  0.0 0.0 copy-start
  0.0 0.0 copy-start.2
  0.0 0.0 copy-start.3
  0.0 0.0 copy-start.1
  0.0 3.0 %collective-permute-start = (bf16[16,1024]{1,0:T(8,128)(2,1)}, bf16[16,1024]{1,0:T(8,128)(2,1)S(1)}, u32[]{:S(2)}, u32[]{:S(2)}) collective-permute-start(bf16[16,1024]{1,0:T(8,128)(2,1)} %refs_3_.1), channel_id=1, source_target_pairs={{0,16},{1,17},{2,18},{3,19},{4,20},{5,21},{6,22},{7,23},{8,24},{9,... | collective-permute-start | bytes 98312 | tf_op jit(solution)/shard_map/ppermute | solution.py:205
  3.0 3.5 %collective-permute-start.5 = (bf16[16,1024]{1,0:T(8,128)(2,1)}, bf16[16,1024]{1,0:T(8,128)(2,1)S(1)}, u32[]{:S(2)}, u32[]{:S(2)}) collective-permute-start(bf16[16,1024]{1,0:T(8,128)(2,1)} %refs_3_.1), channel_id=1, source_target_pairs={{0,5},{1,4},{2,7},{3,6},{4,1},{5,0},{6,3},{7,2},{8,14},{9,15},{10,... | collective-permute-start | bytes 98312 | tf_op jit(solution)/shard_map/ppermute | solution.py:205
  6.6 0.3 %collective-permute-start.6 = (bf16[16,1024]{1,0:T(8,128)(2,1)}, bf16[16,1024]{1,0:T(8,128)(2,1)S(1)}, u32[]{:S(2)}, u32[]{:S(2)}) collective-permute-start(bf16[16,1024]{1,0:T(8,128)(2,1)} %refs_3_.1), channel_id=1, source_target_pairs={{0,4},{1,5},{2,6},{3,7},{4,0},{5,1},{6,2},{7,3},{8,12},{9,13},{10,... | collective-permute-start | bytes 98312 | tf_op jit(solution)/shard_map/ppermute | solution.py:205
  6.9 0.5 %collective-permute-start.7 = (bf16[16,1024]{1,0:T(8,128)(2,1)}, bf16[16,1024]{1,0:T(8,128)(2,1)S(1)}, u32[]{:S(2)}, u32[]{:S(2)}) collective-permute-start(bf16[16,1024]{1,0:T(8,128)(2,1)} %refs_3_.1), channel_id=1, source_target_pairs={{0,1},{1,0},{2,3},{3,2},{4,5},{5,4},{6,7},{7,6},{8,10},{9,11},{10,... | collective-permute-start | bytes 98312 | tf_op jit(solution)/shard_map/ppermute | solution.py:205
  7.4 0.0 collective-permute-done.refs_0_
  7.4 0.0 copy-done
  7.4 0.1 collective-permute-start.1
  7.5 0.0 copy-done.2
  7.5 0.0 copy-done.3
  7.5 0.1 pad_add_fusion.index_ref
  8.3 0.7 %collective-permute-done.5.refs_0_ = bf16[16,1024]{1,0:T(8,128)(2,1)S(1)} collective-permute-done((bf16[16,1024]{1,0:T(8,128)(2,1)}, bf16[16,1024]{1,0:T(8,128)(2,1)S(1)}, u32[]{:S(2)}, u32[]{:S(2)}) %collective-permute-start.5) | collective-permute-done | bytes 32800 | tf_op jit(solution)/shard_map/ppermute | solution.py:205
  8.9 2.6 %collective-permute-done.6.refs_1_ = bf16[16,1024]{1,0:T(8,128)(2,1)S(1)} collective-permute-done((bf16[16,1024]{1,0:T(8,128)(2,1)}, bf16[16,1024]{1,0:T(8,128)(2,1)S(1)}, u32[]{:S(2)}, u32[]{:S(2)}) %collective-permute-start.6) | collective-permute-done | bytes 32800 | tf_op jit(solution)/shard_map/ppermute | solution.py:205
  11.6 0.0 collective-permute-done.7.refs_2_
  11.6 1.6 %collective-permute-start.8 = (bf16[4,16,1024]{2,1,0:T(8,128)(2,1)S(1)}, bf16[4,16,1024]{2,1,0:T(8,128)(2,1)S(1)}, u32[]{:S(2)}, u32[]{:S(2)}) collective-permute-start(bf16[4,16,1024]{2,1,0:T(8,128)(2,1)S(1)} %stack_pieces.3.refs_0_), channel_id=1, source_target_pairs={{0,2},{1,3},{2,0},{3,1},{4,6},{5,7},{6,4},{7,5},{8,9},{9,8},{10,11... | collective-permute-start | bytes 393224 | tf_op jit(solution)/shard_map/ppermute | solution.py:205
  13.3 0.0 collective-permute-done.1.refs_1_
  13.3 0.0 copy-done.1
  13.3 1.4 %direct_blocks.1 = (f32[2,16,1024]{2,1,0:T(8,128)S(1)}, s16[2,16,1152]{2,1,0:T(8,128)(2,1)S(1)}, s16[2,16,1152]{2,1,0:T(8,128)(2,1)S(1)}, s16[2,16,1152]{2,1,0:T(8,128)(2,1)S(1)}) custom-call(s32[16]{0:T(128)S(1)} %pad_add_fusion.index_ref, s32[1,1]{1,0:T(1,128)S(6)} %copy.6.count_ref, bf16[1,1,8,512,512]{4,3,2,1,0:T(8,128)(2,1)S(1)} %copy-done.1, ...), custom_call_target="tpu_custom_call" | custom-call | flops 6710886400 | bytes 33554432 | tf_op jit(solution)/shard_map/direct_blocks/pallas_call | solution.py:235
  14.7 1.1 %collective-permute-start.2 = (s16[2,16,1152]{2,1,0:T(8,128)(2,1)S(1)}, s16[2,16,1152]{2,1,0:T(8,128)(2,1)S(1)}, u32[]{:S(2)}, u32[]{:S(2)}) collective-permute-start(s16[2,16,1152]{2,1,0:T(8,128)(2,1)S(1)} %get-tuple-element.17), channel_id=1, source_target_pairs={{0,3},{1,2},{2,1},{3,0},{4,7},{5,6},{6,5},{7,4},{8,13},{9,12},{10,... | collective-permute-start | bytes 221192 | tf_op jit(solution)/shard_map/ppermute | solution.py:205
  15.8 0.9 %collective-permute-start.3 = (s16[2,16,1152]{2,1,0:T(8,128)(2,1)S(1)}, s16[2,16,1152]{2,1,0:T(8,128)(2,1)S(1)}, u32[]{:S(2)}, u32[]{:S(2)}) collective-permute-start(s16[2,16,1152]{2,1,0:T(8,128)(2,1)S(1)} %get-tuple-element.18), channel_id=1, source_target_pairs={{0,1},{1,0},{2,3},{3,2},{4,5},{5,4},{6,7},{7,6},{8,12},{9,13},{10,... | collective-permute-start | bytes 221192 | tf_op jit(solution)/shard_map/ppermute | solution.py:205
  16.6 1.6 %collective-permute-start.4 = (s16[2,16,1152]{2,1,0:T(8,128)(2,1)S(1)}, s16[2,16,1152]{2,1,0:T(8,128)(2,1)S(1)}, u32[]{:S(2)}, u32[]{:S(2)}) collective-permute-start(s16[2,16,1152]{2,1,0:T(8,128)(2,1)S(1)} %get-tuple-element.19), channel_id=1, source_target_pairs={{0,2},{1,3},{2,0},{3,1},{4,6},{5,7},{6,4},{7,5},{8,9},{9,8},{10,11... | collective-permute-start | bytes 221192 | tf_op jit(solution)/shard_map/ppermute | solution.py:205
  18.2 0.0 collective-permute-done.8.refs_1_
  18.2 1.1 %mirror_blocks.1 = (f32[1,16,1024]{2,1,0:T(8,128)S(1)}, s16[1,16,1152]{2,1,0:T(8,128)(2,1)S(1)}, s16[1,16,1152]{2,1,0:T(8,128)(2,1)S(1)}, s16[1,16,1152]{2,1,0:T(8,128)(2,1)S(1)}) custom-call(s32[16]{0:T(128)S(1)} %pad_add_fusion.index_ref, s32[1,1]{1,0:T(1,128)S(6)} %copy.6.count_ref, bf16[1,1,8,512,512]{4,3,2,1,0:T(8,128)(2,1)S(1)} %copy-done.1, ...), custom_call_target="tpu_custom_call" | custom-call | flops 6710886400 | bytes 33554432 | tf_op jit(solution)/shard_map/mirror_blocks/pallas_call | solution.py:235
  19.3 0.1 collective-permute-start.10
  19.4 0.6 %collective-permute-start.11 = (s16[1,16,1152]{2,1,0:T(8,128)(2,1)S(1)}, s16[1,16,1152]{2,1,0:T(8,128)(2,1)S(1)}, u32[]{:S(2)}, u32[]{:S(2)}) collective-permute-start(s16[1,16,1152]{2,1,0:T(8,128)(2,1)S(1)} %get-tuple-element.25), channel_id=1, source_target_pairs={{0,16},{1,17},{2,18},{3,19},{4,20},{5,21},{6,22},{7,23},{8,24},{9,... | collective-permute-start | bytes 110600 | tf_op jit(solution)/shard_map/ppermute | solution.py:205
  20.0 0.3 %collective-permute-done.2.refs_0_ = s16[2,16,1152]{2,1,0:T(8,128)(2,1)S(1)} collective-permute-done((s16[2,16,1152]{2,1,0:T(8,128)(2,1)S(1)}, s16[2,16,1152]{2,1,0:T(8,128)(2,1)S(1)}, u32[]{:S(2)}, u32[]{:S(2)}) %collective-permute-start.2) | collective-permute-done | bytes 73760 | tf_op jit(solution)/shard_map/ppermute | solution.py:205
  20.3 0.6 %collective-permute-done.3.refs_1_ = s16[2,16,1152]{2,1,0:T(8,128)(2,1)S(1)} collective-permute-done((s16[2,16,1152]{2,1,0:T(8,128)(2,1)S(1)}, s16[2,16,1152]{2,1,0:T(8,128)(2,1)S(1)}, u32[]{:S(2)}, u32[]{:S(2)}) %collective-permute-start.3) | collective-permute-done | bytes 73760 | tf_op jit(solution)/shard_map/ppermute | solution.py:205
  20.9 0.1 collective-permute-done.4.refs_2_
  21.0 0.2 add_near.1
  21.2 2.1 %collective-permute-start.9 = (s16[1,16,1152]{2,1,0:T(8,128)(2,1)S(1)}, s16[1,16,1152]{2,1,0:T(8,128)(2,1)S(1)}, u32[]{:S(2)}, u32[]{:S(2)}) collective-permute-start(s16[1,16,1152]{2,1,0:T(8,128)(2,1)S(1)} %get-tuple-element.23), channel_id=1, source_target_pairs={{0,4},{1,5},{2,6},{3,7},{4,0},{5,1},{6,2},{7,3},{8,10},{9,11},{10,... | collective-permute-start | bytes 110600 | tf_op jit(solution)/shard_map/ppermute | solution.py:205
  23.3 0.0 collective-permute-start.12
  23.3 0.0 collective-permute-done.10.refs_3_
  23.3 0.3 collective-permute-done.11.refs_4_
  23.6 2.6 %collective-permute-done.9.refs_2_ = s16[1,16,1152]{2,1,0:T(8,128)(2,1)S(1)} collective-permute-done((s16[1,16,1152]{2,1,0:T(8,128)(2,1)S(1)}, s16[1,16,1152]{2,1,0:T(8,128)(2,1)S(1)}, u32[]{:S(2)}, u32[]{:S(2)}) %collective-permute-start.9) | collective-permute-done | bytes 36896 | tf_op jit(solution)/shard_map/ppermute | solution.py:205
  26.1 0.0 collective-permute-done.12.refs_5_
  26.1 0.7 %add_up.1 = f32[16,1024]{1,0:T(8,128)} custom-call(f32[1,16,1024]{2,1,0:T(8,128)S(1)} %get-tuple-element.21.refs_0_, f32[1,16,1024]{2,1,0:T(8,128)S(1)} %get-tuple-element.22.refs_1_, s16[1,16,1152]{2,1,0:T(8,128)(2,1)S(1)} %collective-permute-done.9.refs_2_, s16[1,16,1152]{2,1,0:T(8,128)(2,1)S(1)} %collective-permute-done.10.refs_3_, ...), custom_call_target="tpu_custom_call" | custom-call | tf_op jit(solution)/shard_map/add_up/pallas_call | solution.py:225
  (3 shorter events, 0.0 us)
Async XLA Ops:
  0.0 7.4 %copy-start = (bf16[16,1024]{1,0:T(8,128)(2,1)S(1)}, bf16[16,1024]{1,0:T(8,128)(2,1)}, u32[]{:S(2)}) copy-start(bf16[16,1024]{1,0:T(8,128)(2,1)} %refs_3_.1) | copy-start | bytes 98308
  0.0 7.5 %copy-start.2 = (s32[1,1,8]{2,1,0:T(1,128)S(1)}, s32[1,1,8]{2,1,0:T(1,128)}, u32[]{:S(2)}) copy-start(s32[1,1,8]{2,1,0:T(1,128)} %param.8) | copy-start | bytes 100
  0.0 7.5 %copy-start.3 = (s32[1,1,8]{2,1,0:T(1,128)S(1)}, s32[1,1,8]{2,1,0:T(1,128)}, u32[]{:S(2)}) copy-start(s32[1,1,8]{2,1,0:T(1,128)} %param.7) | copy-start | bytes 100
  0.0 13.3 %copy-start.1 = (bf16[1,1,8,512,512]{4,3,2,1,0:T(8,128)(2,1)S(1)}, bf16[1,1,8,512,512]{4,3,2,1,0:T(8,128)(2,1)}, u32[]{:S(2)}) copy-start(bf16[1,1,8,512,512]{4,3,2,1,0:T(8,128)(2,1)} %tiles.3) | copy-start | bytes 12582916
  0.0 7.4 %collective-permute-start = (bf16[16,1024]{1,0:T(8,128)(2,1)}, bf16[16,1024]{1,0:T(8,128)(2,1)S(1)}, u32[]{:S(2)}, u32[]{:S(2)}) collective-permute-start(bf16[16,1024]{1,0:T(8,128)(2,1)} %refs_3_.1), channel_id=1, source_target_pairs={{0,16},{1,17},{2,18},{3,19},{4,20},{5,21},{6,22},{7,23},{8,24},{9,... | collective-permute-start | bytes 98312 | tf_op jit(solution)/shard_map/ppermute | solution.py:205
  3.0 5.9 %collective-permute-start.5 = (bf16[16,1024]{1,0:T(8,128)(2,1)}, bf16[16,1024]{1,0:T(8,128)(2,1)S(1)}, u32[]{:S(2)}, u32[]{:S(2)}) collective-permute-start(bf16[16,1024]{1,0:T(8,128)(2,1)} %refs_3_.1), channel_id=1, source_target_pairs={{0,5},{1,4},{2,7},{3,6},{4,1},{5,0},{6,3},{7,2},{8,14},{9,15},{10,... | collective-permute-start | bytes 98312 | tf_op jit(solution)/shard_map/ppermute | solution.py:205
  6.6 5.0 %collective-permute-start.6 = (bf16[16,1024]{1,0:T(8,128)(2,1)}, bf16[16,1024]{1,0:T(8,128)(2,1)S(1)}, u32[]{:S(2)}, u32[]{:S(2)}) collective-permute-start(bf16[16,1024]{1,0:T(8,128)(2,1)} %refs_3_.1), channel_id=1, source_target_pairs={{0,4},{1,5},{2,6},{3,7},{4,0},{5,1},{6,2},{7,3},{8,12},{9,13},{10,... | collective-permute-start | bytes 98312 | tf_op jit(solution)/shard_map/ppermute | solution.py:205
  6.9 4.7 %collective-permute-start.7 = (bf16[16,1024]{1,0:T(8,128)(2,1)}, bf16[16,1024]{1,0:T(8,128)(2,1)S(1)}, u32[]{:S(2)}, u32[]{:S(2)}) collective-permute-start(bf16[16,1024]{1,0:T(8,128)(2,1)} %refs_3_.1), channel_id=1, source_target_pairs={{0,1},{1,0},{2,3},{3,2},{4,5},{5,4},{6,7},{7,6},{8,10},{9,11},{10,... | collective-permute-start | bytes 98312 | tf_op jit(solution)/shard_map/ppermute | solution.py:205
  7.4 5.8 %collective-permute-start.1 = (bf16[2,16,1024]{2,1,0:T(8,128)(2,1)S(1)}, bf16[2,16,1024]{2,1,0:T(8,128)(2,1)S(1)}, u32[]{:S(2)}, u32[]{:S(2)}) collective-permute-start(bf16[2,16,1024]{2,1,0:T(8,128)(2,1)S(1)} %stack_pieces.2.refs_0_), channel_id=1, source_target_pairs={{0,8},{1,9},{2,10},{3,11},{4,12},{5,13},{6,14},{7,15},{8,0},{9,1},... | collective-permute-start | bytes 196616 | tf_op jit(solution)/shard_map/ppermute | solution.py:205
  11.6 6.6 %collective-permute-start.8 = (bf16[4,16,1024]{2,1,0:T(8,128)(2,1)S(1)}, bf16[4,16,1024]{2,1,0:T(8,128)(2,1)S(1)}, u32[]{:S(2)}, u32[]{:S(2)}) collective-permute-start(bf16[4,16,1024]{2,1,0:T(8,128)(2,1)S(1)} %stack_pieces.3.refs_0_), channel_id=1, source_target_pairs={{0,2},{1,3},{2,0},{3,1},{4,6},{5,7},{6,4},{7,5},{8,9},{9,8},{10,11... | collective-permute-start | bytes 393224 | tf_op jit(solution)/shard_map/ppermute | solution.py:205
  14.7 5.6 %collective-permute-start.2 = (s16[2,16,1152]{2,1,0:T(8,128)(2,1)S(1)}, s16[2,16,1152]{2,1,0:T(8,128)(2,1)S(1)}, u32[]{:S(2)}, u32[]{:S(2)}) collective-permute-start(s16[2,16,1152]{2,1,0:T(8,128)(2,1)S(1)} %get-tuple-element.17), channel_id=1, source_target_pairs={{0,3},{1,2},{2,1},{3,0},{4,7},{5,6},{6,5},{7,4},{8,13},{9,12},{10,... | collective-permute-start | bytes 221192 | tf_op jit(solution)/shard_map/ppermute | solution.py:205
  15.8 5.1 %collective-permute-start.3 = (s16[2,16,1152]{2,1,0:T(8,128)(2,1)S(1)}, s16[2,16,1152]{2,1,0:T(8,128)(2,1)S(1)}, u32[]{:S(2)}, u32[]{:S(2)}) collective-permute-start(s16[2,16,1152]{2,1,0:T(8,128)(2,1)S(1)} %get-tuple-element.18), channel_id=1, source_target_pairs={{0,1},{1,0},{2,3},{3,2},{4,5},{5,4},{6,7},{7,6},{8,12},{9,13},{10,... | collective-permute-start | bytes 221192 | tf_op jit(solution)/shard_map/ppermute | solution.py:205
  16.6 4.4 %collective-permute-start.4 = (s16[2,16,1152]{2,1,0:T(8,128)(2,1)S(1)}, s16[2,16,1152]{2,1,0:T(8,128)(2,1)S(1)}, u32[]{:S(2)}, u32[]{:S(2)}) collective-permute-start(s16[2,16,1152]{2,1,0:T(8,128)(2,1)S(1)} %get-tuple-element.19), channel_id=1, source_target_pairs={{0,2},{1,3},{2,0},{3,1},{4,6},{5,7},{6,4},{7,5},{8,9},{9,8},{10,11... | collective-permute-start | bytes 221192 | tf_op jit(solution)/shard_map/ppermute | solution.py:205
  19.3 4.0 %collective-permute-start.10 = (s16[1,16,1152]{2,1,0:T(8,128)(2,1)S(1)}, s16[1,16,1152]{2,1,0:T(8,128)(2,1)S(1)}, u32[]{:S(2)}, u32[]{:S(2)}) collective-permute-start(s16[1,16,1152]{2,1,0:T(8,128)(2,1)S(1)} %get-tuple-element.24), channel_id=1, source_target_pairs={{0,24},{1,25},{2,26},{3,27},{4,28},{5,29},{6,30},{7,31},{8,16},{9,... | collective-permute-start | bytes 110600 | tf_op jit(solution)/shard_map/ppermute | solution.py:205
  19.4 4.2 %collective-permute-start.11 = (s16[1,16,1152]{2,1,0:T(8,128)(2,1)S(1)}, s16[1,16,1152]{2,1,0:T(8,128)(2,1)S(1)}, u32[]{:S(2)}, u32[]{:S(2)}) collective-permute-start(s16[1,16,1152]{2,1,0:T(8,128)(2,1)S(1)} %get-tuple-element.25), channel_id=1, source_target_pairs={{0,16},{1,17},{2,18},{3,19},{4,20},{5,21},{6,22},{7,23},{8,24},{9,... | collective-permute-start | bytes 110600 | tf_op jit(solution)/shard_map/ppermute | solution.py:205
  21.2 4.9 %collective-permute-start.9 = (s16[1,16,1152]{2,1,0:T(8,128)(2,1)S(1)}, s16[1,16,1152]{2,1,0:T(8,128)(2,1)S(1)}, u32[]{:S(2)}, u32[]{:S(2)}) collective-permute-start(s16[1,16,1152]{2,1,0:T(8,128)(2,1)S(1)} %get-tuple-element.23), channel_id=1, source_target_pairs={{0,4},{1,5},{2,6},{3,7},{4,0},{5,1},{6,2},{7,3},{8,10},{9,11},{10,... | collective-permute-start | bytes 110600 | tf_op jit(solution)/shard_map/ppermute | solution.py:205
  23.3 2.8 %collective-permute-start.12 = (s16[1,16,1152]{2,1,0:T(8,128)(2,1)S(1)}, s16[1,16,1152]{2,1,0:T(8,128)(2,1)S(1)}, u32[]{:S(2)}, u32[]{:S(2)}) collective-permute-start(s16[1,16,1152]{2,1,0:T(8,128)(2,1)S(1)} %get-tuple-element.26), channel_id=1, source_target_pairs={{0,8},{1,9},{2,10},{3,11},{4,12},{5,13},{6,14},{7,15},{8,0},{9,1},... | collective-permute-start | bytes 110600 | tf_op jit(solution)/shard_map/ppermute | solution.py:205
